TPU v7x, 32 devices: a whole 2x2x4 slice. The times are simulated.
32 devices in a mesh: dp: 8 (over z, x), tensor: 4 (over y, core).
Axes of the slice: x: 2, y: 2, z: 4, core: 2. Of those that a mesh axis runs over, the one named last changes fastest.
Arguments:
- tokens: bfloat16 [32768, 256], P('dp'), may hold values from -6 to 6
- positions: bfloat16 [32768, 256], P('dp'), may hold values from -1 to 1
- segment_ids: int32 [8, 4096], P('dp'), may hold values from 0 to 4, as said below
- pad_flags: int32 [8, 4096], P('dp'), may hold values from 0 to 1, as said below
- cotangent: bfloat16 [32768, 256], P('dp'), may hold values from -6 to 6
- inward: float32 [3, 256, 256], P(None, 'dp', 'tensor'), may hold values from -0.375 to 0.375
- outward: float32 [256, 256], P('tensor', 'dp'), may hold values from -1 to 1
- upward: float32 [256, 2048], P('dp', 'tensor'), may hold values from -0.375 to 0.375
- downward: float32 [2048, 256], P('tensor', 'dp'), may hold values from -0.1875 to 0.1875
- vectors: float32 [6, 256], P(None, 'dp')
- offsets: float32 [2, 256], P(None, ('tensor', 'dp')), may hold values from -4 to 4
- shifts: float32 [2048], P(('tensor', 'dp')), may hold values from -4 to 4
- first_inward: float32 [3, 256, 256], P(None, 'dp', 'tensor'), may hold values from -1536 to 1536
- first_outward: float32 [256, 256], P('tensor', 'dp'), may hold values from -224 to 224
- first_upward: float32 [256, 2048], P('dp', 'tensor'), may hold values from -224 to 224
- first_downward: float32 [2048, 256], P('tensor', 'dp'), may hold values from -512 to 512
- first_vectors: float32 [6, 256], P(None, 'dp'), may hold values from -768 to 768
- first_offsets: float32 [2, 256], P(None, ('tensor', 'dp')), may hold values from -1536 to 1536
- first_shifts: float32 [2048], P(('tensor', 'dp')), may hold values from -224 to 224
- second_inward: float32 [3, 256, 256], P(None, 'dp', 'tensor'), may hold values from 73728 to 294912
- second_outward: float32 [256, 256], P('tensor', 'dp'), may hold values from 1310.72 to 5242.88
- second_upward: float32 [256, 2048], P('dp', 'tensor'), may hold values from 1310.72 to 5242.88
- second_downward: float32 [2048, 256], P('tensor', 'dp'), may hold values from 6553.6 to 26214.4
- second_vectors: float32 [6, 256], P(None, 'dp'), may hold values from 16384 to 65536
- second_offsets: float32 [2, 256], P(None, ('tensor', 'dp')), may hold values from 73728 to 294912
- second_shifts: float32 [2048], P(('tensor', 'dp')), may hold values from 1310.72 to 5242.88
Outputs:
- encoded: bfloat16 [32768, 256], P('dp')
- token_grad: float32 [32768, 256], P('dp')
- grad_inward: float32 [3, 256, 256], P(None, 'dp', 'tensor')
- grad_outward: float32 [256, 256], P('tensor', 'dp')
- grad_upward: float32 [256, 2048], P('dp', 'tensor')
- grad_downward: float32 [2048, 256], P('tensor', 'dp')
- grad_vectors: float32 [6, 256], P(None, 'dp')
- grad_offsets: float32 [2, 256], P(None, ('tensor', 'dp'))
- grad_shifts: float32 [2048], P(('tensor', 'dp'))
- updated_inward: float32 [3, 256, 256], P(None, 'dp', 'tensor')
- updated_outward: float32 [256, 256], P('tensor', 'dp')
- updated_upward: float32 [256, 2048], P('dp', 'tensor')
- updated_downward: float32 [2048, 256], P('tensor', 'dp')
- updated_vectors: float32 [6, 256], P(None, 'dp')
- updated_offsets: float32 [2, 256], P(None, ('tensor', 'dp'))
- updated_shifts: float32 [2048], P(('tensor', 'dp'))
- lowered_inward: bfloat16 [3, 256, 256], P(None, 'dp', 'tensor')
- lowered_outward: bfloat16 [256, 256], P('tensor', 'dp')
- lowered_upward: bfloat16 [256, 2048], P('dp', 'tensor')
- lowered_downward: bfloat16 [2048, 256], P('tensor', 'dp')
- momentum_inward: float32 [3, 256, 256], P(None, 'dp', 'tensor')
- momentum_outward: float32 [256, 256], P('tensor', 'dp')
- momentum_upward: float32 [256, 2048], P('dp', 'tensor')
- momentum_downward: float32 [2048, 256], P('tensor', 'dp')
- momentum_vectors: float32 [6, 256], P(None, 'dp')
- momentum_offsets: float32 [2, 256], P(None, ('tensor', 'dp'))
- momentum_shifts: float32 [2048], P(('tensor', 'dp'))
- variance_inward: float32 [3, 256, 256], P(None, 'dp', 'tensor')
- variance_outward: float32 [256, 256], P('tensor', 'dp')
- variance_upward: float32 [256, 2048], P('dp', 'tensor')
- variance_downward: float32 [2048, 256], P('tensor', 'dp')
- variance_vectors: float32 [6, 256], P(None, 'dp')
- variance_offsets: float32 [2, 256], P(None, ('tensor', 'dp'))
- variance_shifts: float32 [2048], P(('tensor', 'dp'))
Inputs may be any that keep to these rules, and one draw needn't show every extreme that they name: `segment_ids`: in every pack the ids never fall and every id from 0 to 4 occurs. `pad_flags`: the first token of every image is never padding.
All inputs are finite; a program needn't handle non-finite values.
Results may differ from a plain program's by a relative error of at most 0.008.
The roundings to bfloat16 on the way count: a program that leaves them out, or rounds other values in their place, can miss the bound.
Values may be sent and summed in bfloat16 or wider, within the bound.
A program may use at most 128 MiB of HBM per device.

v0:
```python
import jax
import jax.numpy as jnp
from jax import lax
from jax.sharding import PartitionSpec as P

HEAD_DIM = 32
STEP = 10
neg_fill = -1e30
norm_eps = 1e-05
beta_one = 0.5
beta_two = 0.5
adam_eps = 1e-08
decay_rate = 0.0001
step_rates = (0.06, 0.15, 0.06, 0.03, 0.1, 0.1, 0.1)
block_limit = 512


def product(left_side, right_side):
    return jnp.dot(left_side, right_side, preferred_element_type=jnp.float32)


def product_left(left_side, right_side):
    return lax.dot_general(
        left_side, right_side, (((0,), (0,)), ((), ())), preferred_element_type=jnp.float32
    )


def product_right(left_side, right_side):
    return lax.dot_general(
        left_side, right_side, (((1,), (1,)), ((), ())), preferred_element_type=jnp.float32
    )


def smooth_unit(values):
    return jax.nn.gelu(values, approximate=False)


def norm_forward(values, gain_row, shift_row):
    center = values - jnp.mean(values, axis=-1, keepdims=True)
    inverse = lax.rsqrt(jnp.mean(center * center, axis=-1, keepdims=True) + norm_eps)
    scaled = center * inverse
    return (scaled * gain_row + shift_row, scaled, inverse)


def norm_backward(upstream, scaled, inverse, gain_row):
    spread = upstream * gain_row
    centred = (
        spread
        - jnp.mean(spread, axis=-1, keepdims=True)
        - scaled * jnp.mean(spread * scaled, axis=-1, keepdims=True)
    )
    return (inverse * centred, jnp.sum(upstream * scaled, axis=0), jnp.sum(upstream, axis=0))


def summed(partial_value):
    return lax.psum(partial_value, "tensor")


def mask_scores(query_block, key_heads, seg_block, segment, key_open):
    scores = jnp.einsum(
        "qhd,khd->hqk", query_block, key_heads, preferred_element_type=jnp.float32
    ) * HEAD_DIM ** (-0.5)
    allowed = (seg_block[:, None] == segment[None, :]) & key_open[None, :]
    return jnp.where(allowed[None], scores, neg_fill)


def attend_forward(queries, key_rows, values, segment, key_open):
    row_count = queries.shape[0]
    block_rows = min(block_limit, row_count)
    heads_here = queries.shape[1] // HEAD_DIM
    key_heads = key_rows.reshape(row_count, heads_here, HEAD_DIM)
    value_heads = values.reshape(row_count, heads_here, HEAD_DIM)

    def one_block(block_index):
        first_row = block_index * block_rows
        query_block = lax.dynamic_slice_in_dim(queries, first_row, block_rows, 0).reshape(
            block_rows, heads_here, HEAD_DIM
        )
        seg_block = lax.dynamic_slice_in_dim(segment, first_row, block_rows, 0)
        scores = mask_scores(query_block, key_heads, seg_block, segment, key_open)
        maxima = jnp.max(scores, axis=-1, keepdims=True)
        exponent = jnp.exp(scores - maxima)
        totals = jnp.sum(exponent, axis=-1, keepdims=True)
        weights = (exponent / totals).astype(jnp.bfloat16)
        context = jnp.einsum(
            "hqk,khd->qhd", weights, value_heads, preferred_element_type=jnp.float32
        )
        return (
            context.reshape(block_rows, heads_here * HEAD_DIM),
            (maxima + jnp.log(totals))[:, :, 0],
        )

    contexts, log_totals = lax.map(one_block, jnp.arange(row_count // block_rows))
    return (contexts.reshape(row_count, heads_here * HEAD_DIM), log_totals)


def attend_backward(queries, key_rows, values, segment, key_open, log_totals, context_grad):
    row_count = queries.shape[0]
    block_rows = min(block_limit, row_count)
    heads_here = queries.shape[1] // HEAD_DIM
    key_heads = key_rows.reshape(row_count, heads_here, HEAD_DIM)
    value_heads = values.reshape(row_count, heads_here, HEAD_DIM)
    scale_value = HEAD_DIM ** (-0.5)

    def one_block(carry, block_index):
        key_total, value_total = carry
        first_row = block_index * block_rows
        query_block = lax.dynamic_slice_in_dim(queries, first_row, block_rows, 0).reshape(
            block_rows, heads_here, HEAD_DIM
        )
        grad_block = lax.dynamic_slice_in_dim(context_grad, first_row, block_rows, 0).reshape(
            block_rows, heads_here, HEAD_DIM
        )
        seg_block = lax.dynamic_slice_in_dim(segment, first_row, block_rows, 0)
        scores = mask_scores(query_block, key_heads, seg_block, segment, key_open)
        probs = jnp.exp(scores - log_totals[block_index][:, :, None])
        prob_grad = jnp.einsum(
            "qhd,khd->hqk", grad_block, value_heads, preferred_element_type=jnp.float32
        )
        delta = jnp.sum(probs * prob_grad, axis=-1, keepdims=True)
        score_grad = (probs * (prob_grad - delta)).astype(jnp.bfloat16)
        query_grad = (
            jnp.einsum("hqk,khd->qhd", score_grad, key_heads, preferred_element_type=jnp.float32)
            * scale_value
        )
        key_total = key_total + jnp.einsum(
            "hqk,qhd->khd", score_grad, query_block, preferred_element_type=jnp.float32
        )
        value_total = value_total + jnp.einsum(
            "hqk,qhd->khd",
            probs.astype(jnp.bfloat16),
            grad_block,
            preferred_element_type=jnp.float32,
        )
        return (
            (key_total, value_total),
            query_grad.astype(jnp.bfloat16).reshape(block_rows, heads_here * HEAD_DIM),
        )

    zeros_init = jnp.zeros((row_count, heads_here, HEAD_DIM), jnp.float32)
    (key_total, value_total), query_grads = lax.scan(
        one_block, (zeros_init, zeros_init), jnp.arange(row_count // block_rows)
    )
    query_grad = query_grads.reshape(row_count, heads_here * HEAD_DIM)
    key_grad = (
        (key_total * scale_value).astype(jnp.bfloat16).reshape(row_count, heads_here * HEAD_DIM)
    )
    value_grad = value_total.astype(jnp.bfloat16).reshape(row_count, heads_here * HEAD_DIM)
    return (query_grad, key_grad, value_grad)


def adamw(master, gradient, old_first, old_second, step_rate):
    momentum = beta_one * old_first + (1.0 - beta_one) * gradient
    variance = beta_two * old_second + (1.0 - beta_two) * gradient * gradient
    normal_step = (
        momentum / (1.0 - beta_one**STEP) / (jnp.sqrt(variance / (1.0 - beta_two**STEP)) + adam_eps)
    )
    return (master - step_rate * (normal_step + decay_rate * master), momentum, variance)


def body(
    tokens,
    positions,
    segment_ids,
    pad_flags,
    cotangent,
    inward,
    outward,
    upward,
    downward,
    vectors,
    offsets,
    shifts,
    first_inward,
    first_outward,
    first_upward,
    first_downward,
    first_vectors,
    first_offsets,
    first_shifts,
    second_inward,
    second_outward,
    second_upward,
    second_downward,
    second_vectors,
    second_offsets,
    second_shifts,
):
    w_inward, w_outward, w_upward, w_downward, vector_low, offset_low, shift_low = (
        lax.all_gather(inward.astype(jnp.bfloat16), "dp", axis=1, tiled=True),
        lax.all_gather(outward.astype(jnp.bfloat16), "dp", axis=1, tiled=True),
        lax.all_gather(upward.astype(jnp.bfloat16), "dp", axis=0, tiled=True),
        lax.all_gather(downward.astype(jnp.bfloat16), "dp", axis=1, tiled=True),
        lax.all_gather(vectors.astype(jnp.bfloat16), "dp", axis=1, tiled=True),
        lax.all_gather(offsets.astype(jnp.bfloat16), "dp", axis=1, tiled=True),
        lax.all_gather(shifts.astype(jnp.bfloat16), "dp", axis=0, tiled=True),
    )
    vector_wide = vector_low.astype(jnp.float32)
    offset_wide = offset_low.astype(jnp.float32)
    shift_wide = shift_low.astype(jnp.float32)
    segment = segment_ids[0]
    key_open = pad_flags[0] == 0
    input_wide = tokens.astype(jnp.float32)
    query_in = (input_wide + positions.astype(jnp.float32)).astype(jnp.bfloat16)
    queries = (product(query_in, w_inward[0]) + offset_wide[0]).astype(jnp.bfloat16)
    key_rows = product(query_in, w_inward[1]).astype(jnp.bfloat16)
    values = (product(tokens, w_inward[2]) + offset_wide[1]).astype(jnp.bfloat16)
    context, log_totals = attend_forward(queries, key_rows, values, segment, key_open)
    context_low = context.astype(jnp.bfloat16)
    first_sum = input_wide + summed(product(context_low, w_outward)) + vector_wide[4]
    normed, scaled_one, inverse_one = norm_forward(first_sum, vector_wide[0], vector_wide[1])
    normed_low = normed.astype(jnp.bfloat16)
    hidden = product(normed_low, w_upward) + shift_wide
    unit_value, unit_back = jax.vjp(smooth_unit, hidden)
    active = unit_value.astype(jnp.bfloat16)
    second_sum = normed + summed(product(active, w_downward)) + vector_wide[5]
    result, scaled_two, inverse_two = norm_forward(second_sum, vector_wide[2], vector_wide[3])
    encoded = result.astype(jnp.bfloat16)
    upstream = cotangent.astype(jnp.float32)
    second_grad, gain_two, shift_two = norm_backward(
        upstream, scaled_two, inverse_two, vector_wide[2]
    )
    down_low = second_grad.astype(jnp.bfloat16)
    grad_downward = product_left(active, down_low)
    hidden_low = unit_back(product_right(down_low, w_downward))[0].astype(jnp.bfloat16)
    grad_upward = product_left(normed_low, hidden_low)
    grad_shifts = jnp.sum(hidden_low.astype(jnp.float32), axis=0)
    normed_grad = second_grad + summed(product_right(hidden_low, w_upward))
    first_grad, gain_one, shift_one = norm_backward(
        normed_grad, scaled_one, inverse_one, vector_wide[0]
    )
    first_low = first_grad.astype(jnp.bfloat16)
    grad_outward = product_left(context_low, first_low)
    context_grad = product_right(first_low, w_outward).astype(jnp.bfloat16)
    query_grad, key_grad, value_grad = attend_backward(
        queries, key_rows, values, segment, key_open, log_totals, context_grad
    )
    grad_inward = jnp.stack(
        [
            product_left(query_in, query_grad),
            product_left(query_in, key_grad),
            product_left(tokens, value_grad),
        ]
    )
    grad_offsets = jnp.stack(
        [
            jnp.sum(query_grad.astype(jnp.float32), axis=0),
            jnp.sum(value_grad.astype(jnp.float32), axis=0),
        ]
    )
    input_part = (
        product_right(query_grad, w_inward[0])
        + product_right(key_grad, w_inward[1])
        + product_right(value_grad, w_inward[2])
    )
    input_grad = first_grad + summed(input_part)
    grad_vectors = jnp.stack(
        [
            gain_one,
            shift_one,
            gain_two,
            shift_two,
            jnp.sum(first_grad, axis=0),
            jnp.sum(second_grad, axis=0),
        ]
    )
    reduced = (
        lax.psum_scatter(grad_inward, "dp", scatter_dimension=1, tiled=True),
        lax.psum_scatter(grad_outward, "dp", scatter_dimension=1, tiled=True),
        lax.psum_scatter(grad_upward, "dp", scatter_dimension=0, tiled=True),
        lax.psum_scatter(grad_downward, "dp", scatter_dimension=1, tiled=True),
        lax.psum_scatter(grad_vectors, "dp", scatter_dimension=1, tiled=True),
        lax.psum_scatter(grad_offsets, "dp", scatter_dimension=1, tiled=True),
        lax.psum_scatter(grad_shifts, "dp", scatter_dimension=0, tiled=True),
    )
    masters = (inward, outward, upward, downward, vectors, offsets, shifts)
    firsts = (
        first_inward,
        first_outward,
        first_upward,
        first_downward,
        first_vectors,
        first_offsets,
        first_shifts,
    )
    seconds = (
        second_inward,
        second_outward,
        second_upward,
        second_downward,
        second_vectors,
        second_offsets,
        second_shifts,
    )
    updated = []
    momenta = []
    variances = []
    for master, gradient, old_first, old_second, step_rate in zip(
        masters, reduced, firsts, seconds, step_rates
    ):
        new_master, momentum, variance = adamw(master, gradient, old_first, old_second, step_rate)
        updated.append(new_master)
        momenta.append(momentum)
        variances.append(variance)
    return (
        encoded,
        input_grad,
        reduced[0],
        reduced[1],
        reduced[2],
        reduced[3],
        reduced[4],
        reduced[5],
        reduced[6],
        updated[0],
        updated[1],
        updated[2],
        updated[3],
        updated[4],
        updated[5],
        updated[6],
        updated[0].astype(jnp.bfloat16),
        updated[1].astype(jnp.bfloat16),
        updated[2].astype(jnp.bfloat16),
        updated[3].astype(jnp.bfloat16),
        momenta[0],
        momenta[1],
        momenta[2],
        momenta[3],
        momenta[4],
        momenta[5],
        momenta[6],
        variances[0],
        variances[1],
        variances[2],
        variances[3],
        variances[4],
        variances[5],
        variances[6],
    )


def solution(mesh):
    in_specs = (
        P("dp", None),
        P("dp", None),
        P("dp", None),
        P("dp", None),
        P("dp", None),
        P(None, "dp", "tensor"),
        P("tensor", "dp"),
        P("dp", "tensor"),
        P("tensor", "dp"),
        P(None, "dp"),
        P(None, ("tensor", "dp")),
        P(("tensor", "dp")),
        P(None, "dp", "tensor"),
        P("tensor", "dp"),
        P("dp", "tensor"),
        P("tensor", "dp"),
        P(None, "dp"),
        P(None, ("tensor", "dp")),
        P(("tensor", "dp")),
        P(None, "dp", "tensor"),
        P("tensor", "dp"),
        P("dp", "tensor"),
        P("tensor", "dp"),
        P(None, "dp"),
        P(None, ("tensor", "dp")),
        P(("tensor", "dp")),
    )
    out_specs = (
        P("dp", None),
        P("dp", None),
        P(None, "dp", "tensor"),
        P("tensor", "dp"),
        P("dp", "tensor"),
        P("tensor", "dp"),
        P(None, "dp"),
        P(None, ("tensor", "dp")),
        P(("tensor", "dp")),
        P(None, "dp", "tensor"),
        P("tensor", "dp"),
        P("dp", "tensor"),
        P("tensor", "dp"),
        P(None, "dp"),
        P(None, ("tensor", "dp")),
        P(("tensor", "dp")),
        P(None, "dp", "tensor"),
        P("tensor", "dp"),
        P("dp", "tensor"),
        P("tensor", "dp"),
        P(None, "dp", "tensor"),
        P("tensor", "dp"),
        P("dp", "tensor"),
        P("tensor", "dp"),
        P(None, "dp"),
        P(None, ("tensor", "dp")),
        P(("tensor", "dp")),
        P(None, "dp", "tensor"),
        P("tensor", "dp"),
        P("dp", "tensor"),
        P("tensor", "dp"),
        P(None, "dp"),
        P(None, ("tensor", "dp")),
        P(("tensor", "dp")),
    )
    return jax.shard_map(body, mesh=mesh, in_specs=in_specs, out_specs=out_specs, check_vma=False)
```

profile of v0, /device:TPU:0, one launch (start us, length us, event | category | flops | bytes accessed | tf_op | source)
XLA Modules:
  0.0 1405.3 jit_solution(3010460021737112204)
XLA Ops:
  8.1 22.1 %all-gather = bf16[8,8,2]{1,2,0:T(2,128)(2,1)S(1)} all-gather(bf16[1,8,2]{1,2,0:T(2,128)(2,1)S(1)} %convert_bitcast_fusion.2), channel_id=1, replica_groups=mesh['dp'=8,'tensor'=4] {'dp'}, dimensions={0}, use_global_device_ids=true | all-gather | bytes 288 | tf_op jit(solution)/shard_map/all_gather | solution.py:195
  32.6 32.5 %all_gather.23 = bf16[64,256]{0,1:T(8,128)(2,1)} all-gather(bf16[64,32]{0,1:T(8,128)(2,1)S(1)} %convert_element_type.133), channel_id=1, replica_groups=mesh['dp'=8,'tensor'=4] {'dp'}, dimensions={1}, use_global_device_ids=true | all-gather | bytes 36864 | tf_op jit(solution)/shard_map/all_gather | solution.py:191
  65.1 30.6 %all_gather.21 = bf16[3,256,64]{2,1,0:T(8,128)(2,1)S(1)} all-gather(bf16[3,32,64]{2,1,0:T(8,128)(2,1)S(1)} %convert_element_type.125), channel_id=1, replica_groups=mesh['dp'=8,'tensor'=4] {'dp'}, dimensions={1}, use_global_device_ids=true | all-gather | bytes 110592 | tf_op jit(solution)/shard_map/all_gather | solution.py:190
  101.7 152.2 %while.27 = (s32[]{:T(128)}, bf16[8,512,64]{1,2,0:T(8,128)(2,1)S(1)}, f32[8,2,512]{2,1,0:T(2,128)}, s32[8]{0:T(128)S(1)}, s32[4096]{0:T(1024)}, /*index=5*/s32[1...) while((s32[]{:T(128)}, ...), condition=%wide.region_3.4_spmd, body=%wide.region_0.3_spmd.sunk | while | flops 591395840 | bytes 60221656 | solution.py:93
  259.9 17.4 %all-reduce = bf16[512]{0:T(512)(128)(2,1)S(1)} all-reduce(bf16[512]{0:T(512)(128)(2,1)S(1)} %dynamic-update-slice), channel_id=1, replica_groups=mesh['dp'=8,'tensor'=4] {'dp'}, use_global_device_ids=true, to_apply=%add | all-reduce | flops 512 | bytes 2048
  277.3 26.0 %all-gather.1 = bf16[8,32,6]{1,2,0:T(8,128)(2,1)S(1)} all-gather(bf16[1,32,6]{1,2,0:T(8,128)(2,1)S(1)} %convert_bitcast_fusion.1), channel_id=1, replica_groups=mesh['dp'=8,'tensor'=4] {'dp'}, dimensions={0}, use_global_device_ids=true | all-gather | bytes 3456 | tf_op jit(solution)/shard_map/all_gather | solution.py:194
  303.4 30.8 %all_gather.27 = bf16[512,256]{0,1:T(8,128)(2,1)S(1)} all-gather(bf16[512,32]{0,1:T(8,128)(2,1)S(1)} %convert_element_type.141), channel_id=1, replica_groups=mesh['dp'=8,'tensor'=4] {'dp'}, dimensions={1}, use_global_device_ids=true | all-gather | bytes 294912 | tf_op jit(solution)/shard_map/all_gather | solution.py:193
  334.2 30.7 %all_gather.25 = bf16[256,512]{1,0:T(8,128)(2,1)S(1)} all-gather(bf16[32,512]{1,0:T(8,128)(2,1)S(1)} %convert_element_type.137), channel_id=1, replica_groups=mesh['dp'=8,'tensor'=4] {'dp'}, dimensions={0}, use_global_device_ids=true | all-gather | bytes 294912 | tf_op jit(solution)/shard_map/all_gather | solution.py:192
  371.5 21.6 %multiply_convert_fusion.1 = (bf16[4096,512]{1,0:T(8,128)(2,1)S(1)}, f32[4096,512]{1,0:T(8,128)}, f32[4096,512]{1,0:T(8,128)}) fusion(f32[512]{0:T(512)S(1)} %convert_element_type.139, bf16[4096,256]{1,0:T(8,128)(2,1)S(1)} %fusion.36, bf16[256,512]{1,0:T(8,128)(2,1)S(1)} %all_gather.25), kind=kOutput, calls=%fused_computation.35 | convolution fusion | flops 1212153856 | bytes 23332864 | tf_op jit(solution)/shard_map/dot_general | solution.py:19
  398.5 82.9 %all-reduce.13.cloned.1.call-done = f32[4096,256]{1,0:T(8,128)} async-done(((f32[4096,256]{1,0:T(8,128)}), f32[4096,256]{1,0:T(8,128)}) %all-reduce.13.cloned.1.call-update) | async-done | bytes 4194320 | tf_op jit(solution)/shard_map/psum | solution.py:56
  520.9 74.9 %all-reduce.15.cloned.1.call-done = f32[4096,256]{1,0:T(8,128)} async-done(((f32[4096,256]{1,0:T(8,128)}), f32[4096,256]{1,0:T(8,128)}) %all-reduce.15.cloned.1.call-update) | async-done | bytes 4194320 | tf_op jit(solution)/shard_map/psum | solution.py:56
  609.9 477.1 %while.28 = (s32[]{:T(128)}, f32[4096,2,32]{0,2,1:T(8,128)S(1)}, f32[4096,2,32]{0,2,1:T(8,128)}, bf16[8,512,64]{1,2,0:T(8,128)(2,1)}, s32[8]{0:T(128)S(1)}, /*in...) while((s32[]{:T(128)}, f32[4096,2,32]{0,2,1:T(8,128)S(1)}, ...), condition=%wide.region_17.18_spmd.clone, body=%wide.region_15.17_spmd.clone.sunk | while | flops 1410399232 | bytes 220977600 | solution.py:141
  637.0 15.4 %multiply_reduce_fusion.7 = (f32[2,512]{1,0:T(2,128)S(1)}, f32[2,512,4096]{2,1,0:T(8,128)}) fusion(f32[2,512,4096]{2,1,0:T(8,128)} %copy-done, f32[2,512]{1,0:T(2,128)S(1)} %dynamic-slice_bitcast_fusion.2, pred[512,4096]{1,0:T(8,128)(4,1)} %compare_and_fusion.5, bf16[512,2,32]{0,2,1:T(8,128)(2,1)} %bitcast.191, ...), kind=kOutput, calls=%fused_computation.13.clone.1 | convolution fusion | flops 289405952 | bytes 36249600 | tf_op jit(solution)/shard_map/while/body/eval_jaxpr/qhd,khd->hqk/dot_general | solution.py:117
  652.4 12.5 multiply_convert_fusion.4
  696.7 15.4 %multiply_reduce_fusion.7 = (f32[2,512]{1,0:T(2,128)S(1)}, f32[2,512,4096]{2,1,0:T(8,128)}) fusion(f32[2,512,4096]{2,1,0:T(8,128)} %copy-done, f32[2,512]{1,0:T(2,128)S(1)} %dynamic-slice_bitcast_fusion.2, pred[512,4096]{1,0:T(8,128)(4,1)} %compare_and_fusion.5, bf16[512,2,32]{0,2,1:T(8,128)(2,1)} %bitcast.191, ...), kind=kOutput, calls=%fused_computation.13.clone.1 | convolution fusion | flops 289405952 | bytes 36249600 | tf_op jit(solution)/shard_map/while/body/eval_jaxpr/qhd,khd->hqk/dot_general | solution.py:117
  712.1 12.5 multiply_convert_fusion.4
  756.3 15.4 %multiply_reduce_fusion.7 = (f32[2,512]{1,0:T(2,128)S(1)}, f32[2,512,4096]{2,1,0:T(8,128)}) fusion(f32[2,512,4096]{2,1,0:T(8,128)} %copy-done, f32[2,512]{1,0:T(2,128)S(1)} %dynamic-slice_bitcast_fusion.2, pred[512,4096]{1,0:T(8,128)(4,1)} %compare_and_fusion.5, bf16[512,2,32]{0,2,1:T(8,128)(2,1)} %bitcast.191, ...), kind=kOutput, calls=%fused_computation.13.clone.1 | convolution fusion | flops 289405952 | bytes 36249600 | tf_op jit(solution)/shard_map/while/body/eval_jaxpr/qhd,khd->hqk/dot_general | solution.py:117
  771.7 12.4 multiply_convert_fusion.4
  815.9 15.4 %multiply_reduce_fusion.7 = (f32[2,512]{1,0:T(2,128)S(1)}, f32[2,512,4096]{2,1,0:T(8,128)}) fusion(f32[2,512,4096]{2,1,0:T(8,128)} %copy-done, f32[2,512]{1,0:T(2,128)S(1)} %dynamic-slice_bitcast_fusion.2, pred[512,4096]{1,0:T(8,128)(4,1)} %compare_and_fusion.5, bf16[512,2,32]{0,2,1:T(8,128)(2,1)} %bitcast.191, ...), kind=kOutput, calls=%fused_computation.13.clone.1 | convolution fusion | flops 289405952 | bytes 36249600 | tf_op jit(solution)/shard_map/while/body/eval_jaxpr/qhd,khd->hqk/dot_general | solution.py:117
  831.3 12.4 multiply_convert_fusion.4
  875.5 15.4 %multiply_reduce_fusion.7 = (f32[2,512]{1,0:T(2,128)S(1)}, f32[2,512,4096]{2,1,0:T(8,128)}) fusion(f32[2,512,4096]{2,1,0:T(8,128)} %copy-done, f32[2,512]{1,0:T(2,128)S(1)} %dynamic-slice_bitcast_fusion.2, pred[512,4096]{1,0:T(8,128)(4,1)} %compare_and_fusion.5, bf16[512,2,32]{0,2,1:T(8,128)(2,1)} %bitcast.191, ...), kind=kOutput, calls=%fused_computation.13.clone.1 | convolution fusion | flops 289405952 | bytes 36249600 | tf_op jit(solution)/shard_map/while/body/eval_jaxpr/qhd,khd->hqk/dot_general | solution.py:117
  890.9 12.4 multiply_convert_fusion.4
  935.1 15.4 %multiply_reduce_fusion.7 = (f32[2,512]{1,0:T(2,128)S(1)}, f32[2,512,4096]{2,1,0:T(8,128)}) fusion(f32[2,512,4096]{2,1,0:T(8,128)} %copy-done, f32[2,512]{1,0:T(2,128)S(1)} %dynamic-slice_bitcast_fusion.2, pred[512,4096]{1,0:T(8,128)(4,1)} %compare_and_fusion.5, bf16[512,2,32]{0,2,1:T(8,128)(2,1)} %bitcast.191, ...), kind=kOutput, calls=%fused_computation.13.clone.1 | convolution fusion | flops 289405952 | bytes 36249600 | tf_op jit(solution)/shard_map/while/body/eval_jaxpr/qhd,khd->hqk/dot_general | solution.py:117
  950.5 12.4 multiply_convert_fusion.4
  994.7 15.4 %multiply_reduce_fusion.7 = (f32[2,512]{1,0:T(2,128)S(1)}, f32[2,512,4096]{2,1,0:T(8,128)}) fusion(f32[2,512,4096]{2,1,0:T(8,128)} %copy-done, f32[2,512]{1,0:T(2,128)S(1)} %dynamic-slice_bitcast_fusion.2, pred[512,4096]{1,0:T(8,128)(4,1)} %compare_and_fusion.5, bf16[512,2,32]{0,2,1:T(8,128)(2,1)} %bitcast.191, ...), kind=kOutput, calls=%fused_computation.13.clone.1 | convolution fusion | flops 289405952 | bytes 36249600 | tf_op jit(solution)/shard_map/while/body/eval_jaxpr/qhd,khd->hqk/dot_general | solution.py:117
  1010.1 12.4 multiply_convert_fusion.4
  1054.2 15.4 %multiply_reduce_fusion.7 = (f32[2,512]{1,0:T(2,128)S(1)}, f32[2,512,4096]{2,1,0:T(8,128)}) fusion(f32[2,512,4096]{2,1,0:T(8,128)} %copy-done, f32[2,512]{1,0:T(2,128)S(1)} %dynamic-slice_bitcast_fusion.2, pred[512,4096]{1,0:T(8,128)(4,1)} %compare_and_fusion.5, bf16[512,2,32]{0,2,1:T(8,128)(2,1)} %bitcast.191, ...), kind=kOutput, calls=%fused_computation.13.clone.1 | convolution fusion | flops 289405952 | bytes 36249600 | tf_op jit(solution)/shard_map/while/body/eval_jaxpr/qhd,khd->hqk/dot_general | solution.py:117
  1119.9 21.4 %all-reduce.4 = (f32[2,64]{1,0:T(2,128)S(1)}, f32[512]{0:T(512)S(1)}) all-reduce(f32[2,64]{1,0:T(2,128)S(1)} %pad_maximum_fusion.1, f32[512]{0:T(512)S(1)} %copy-done.57), channel_id=7, replica_groups=mesh['dp'=8,'tensor'=4] {'dp'}, use_global_device_ids=true, to_apply=%region_32.33.clone | all-reduce | flops 640 | bytes 5120
  1142.6 23.4 %reduce-scatter.14.cloned.1.call-done = f32[32,6]{1,0:T(8,128)} async-done(((f32[256,6]{1,0:T(8,128)}), f32[32,6]{1,0:T(8,128)}) %reduce-scatter.14.cloned.1.call-update) | async-done | bytes 784
  1167.4 62.7 %reduce-scatter.8.cloned.1.call-done = f32[64,32]{0,1:T(8,128)} async-done(((f32[64,256]{0,1:T(8,128)}), f32[64,32]{0,1:T(8,128)}) %reduce-scatter.8.cloned.1.call-update) | async-done | bytes 8208 | tf_op jit(solution)/shard_map/reduce_scatter | solution.py:269
  1231.5 73.8 %all-reduce.19.cloned.1.call-done = f32[3,256,64]{2,0,1:T(4,128)} async-done(((f32[3,256,64]{2,0,1:T(4,128)}), f32[3,256,64]{2,0,1:T(4,128)}) %all-reduce.19.cloned.1.call-update) | async-done | bytes 196624
  1306.9 85.6 %all-reduce.17.cloned.1.call-done = f32[4096,256]{1,0:T(8,128)} async-done(((f32[4096,256]{1,0:T(8,128)}), f32[4096,256]{1,0:T(8,128)}) %all-reduce.17.cloned.1.call-update) | async-done | bytes 4194320 | tf_op jit(solution)/shard_map/psum | solution.py:56
  (473 shorter events, 513.7 us)
Async XLA Ops:
  7.2 91.4 %copy-start.12 = (bf16[4096,256]{1,0:T(8,128)(2,1)S(1)}, bf16[4096,256]{1,0:T(8,128)(2,1)}, u32[]{:S(2)}) copy-start(bf16[4096,256]{1,0:T(8,128)(2,1)} %param.30) | copy-start | bytes 6291460
  7.2 357.7 %all-reduce.11.cloned.1.call-start = ((), (), s32[]{:S(2)}) async-start(), calls=%async_computation.4 | async-start | bytes 8388608 | tf_op jit(solution)/shard_map/psum | solution.py:56
  101.7 153.8 %copy-start.29 = (bf16[64,256]{0,1:T(8,128)(2,1)S(1)}, bf16[64,256]{0,1:T(8,128)(2,1)}, u32[]{:S(2)}) copy-start(bf16[64,256]{0,1:T(8,128)(2,1)} %all_gather.23) | copy-start | bytes 98308
  255.5 21.8 %copy-start.46 = (f32[6,32]{1,0:T(8,128)S(1)}, f32[6,32]{1,0:T(8,128)}, u32[]{:S(2)}) copy-start(f32[6,32]{1,0:T(8,128)} %param.39) | copy-start | bytes 2308
  255.5 47.9 %copy-start.33 = (f32[32,512]{1,0:T(8,128)S(1)}, f32[32,512]{1,0:T(8,128)}, u32[]{:S(2)}) copy-start(f32[32,512]{1,0:T(8,128)} %param.37) | copy-start | bytes 196612
  255.5 47.9 %copy-start.31 = (f32[512,32]{0,1:T(8,128)S(1)}, f32[512,32]{0,1:T(8,128)}, u32[]{:S(2)}) copy-start(f32[512,32]{0,1:T(8,128)} %param.38) | copy-start | bytes 196612
  255.5 109.5 %copy-start.13 = (bf16[4096,256]{1,0:T(8,128)(2,1)S(1)}, bf16[4096,256]{1,0:T(8,128)(2,1)}, u32[]{:S(2)}) copy-start(bf16[4096,256]{1,0:T(8,128)(2,1)} %param.30) | copy-start | bytes 6291460
  258.3 223.1 %all-reduce.13.cloned.1.call-start = ((), (), s32[]{:S(2)}) async-start(), calls=%async_computation.5 | async-start | bytes 8388608 | tf_op jit(solution)/shard_map/psum | solution.py:56
  371.5 21.6 %copy-start.24 = (bf16[4096,256]{1,0:T(8,128)(2,1)}, bf16[4096,256]{1,0:T(8,128)(2,1)S(1)}, u32[]{:S(2)}) copy-start(bf16[4096,256]{1,0:T(8,128)(2,1)S(1)} %fusion.36) | copy-start | bytes 6291460
  398.5 197.3 %all-reduce.15.cloned.1.call-start = ((), (), s32[]{:S(2)}) async-start(), calls=%async_computation.6 | async-start | bytes 8388608 | tf_op jit(solution)/shard_map/psum | solution.py:56
  510.0 606.4 %reduce-scatter.12.cloned.1.call-start = ((), (), s32[]{:S(2)}) async-start(), calls=%async_computation.10 | async-start | bytes 589824 | tf_op jit(solution)/shard_map/reduce_scatter | solution.py:271
  515.7 602.4 %reduce-scatter.10.cloned.1.call-start = ((), (), s32[]{:S(2)}) async-start(), calls=%async_computation.9 | async-start | bytes 589824 | tf_op jit(solution)/shard_map/reduce_scatter | solution.py:270
  520.9 645.1 %reduce-scatter.14.cloned.1.call-start = ((), (), s32[]{:S(2)}) async-start(), calls=%async_computation.11 | async-start | bytes 147456
  1104.9 125.2 %reduce-scatter.8.cloned.1.call-start = ((), (), s32[]{:S(2)}) async-start(), calls=%async_computation.8 | async-start | bytes 147456 | tf_op jit(solution)/shard_map/reduce_scatter | solution.py:269
  1105.7 199.7 %all-reduce.19.cloned.1.call-start = ((), (), s32[]{:S(2)}) async-start(), calls=%async_computation.12 | async-start | bytes 1048576
  1109.0 283.5 %all-reduce.17.cloned.1.call-start = ((), (), s32[]{:S(2)}) async-start(), calls=%async_computation.7 | async-start | bytes 8388608 | tf_op jit(solution)/shard_map/psum | solution.py:56
  1114.1 27.2 %copy-start.62 = (f32[64]{0:T(128)S(1)}, f32[64]{0:T(128)}, u32[]{:S(2)}) copy-start(f32[64]{0:T(128)} %param.41) | copy-start | bytes 772
  1114.1 27.2 %copy-start.63 = (f32[64]{0:T(128)S(1)}, f32[64]{0:T(128)}, u32[]{:S(2)}) copy-start(f32[64]{0:T(128)} %param.48) | copy-start | bytes 772
  1114.1 27.2 %copy-start.64 = (f32[64]{0:T(128)S(1)}, f32[64]{0:T(128)}, u32[]{:S(2)}) copy-start(f32[64]{0:T(128)} %param.55) | copy-start | bytes 772
  1114.1 27.8 %copy-start.58 = (f32[2,8]{1,0:T(2,128)S(1)}, f32[2,8]{1,0:T(2,128)}, u32[]{:S(2)}) copy-start(f32[2,8]{1,0:T(2,128)} %param.40) | copy-start | bytes 196
  1114.1 27.8 %copy-start.59 = (f32[2,8]{1,0:T(2,128)S(1)}, f32[2,8]{1,0:T(2,128)}, u32[]{:S(2)}) copy-start(f32[2,8]{1,0:T(2,128)} %param.47) | copy-start | bytes 196
  1114.1 27.7 %copy-start.60 = (f32[2,8]{1,0:T(2,128)S(1)}, f32[2,8]{1,0:T(2,128)}, u32[]{:S(2)}) copy-start(f32[2,8]{1,0:T(2,128)} %param.54) | copy-start | bytes 196
  1114.1 52.6 %copy-start.47 = (f32[6,32]{1,0:T(8,128)S(1)}, f32[6,32]{1,0:T(8,128)}, u32[]{:S(2)}) copy-start(f32[6,32]{1,0:T(8,128)} %param.39) | copy-start | bytes 2308
  1114.2 52.6 %copy-start.53 = (f32[6,32]{1,0:T(8,128)S(1)}, f32[6,32]{1,0:T(8,128)}, u32[]{:S(2)}) copy-start(f32[6,32]{1,0:T(8,128)} %param.46) | copy-start | bytes 2308
  1114.2 52.6 %copy-start.54 = (f32[6,32]{1,0:T(8,128)S(1)}, f32[6,32]{1,0:T(8,128)}, u32[]{:S(2)}) copy-start(f32[6,32]{1,0:T(8,128)} %param.53) | copy-start | bytes 2308
  1114.2 116.0 %copy-start.40 = (f32[64,32]{0,1:T(8,128)S(1)}, f32[64,32]{0,1:T(8,128)}, u32[]{:S(2)}) copy-start(f32[64,32]{0,1:T(8,128)} %param.36) | copy-start | bytes 24580
  1114.2 116.0 %copy-start.43 = (f32[64,32]{0,1:T(8,128)S(1)}, f32[64,32]{0,1:T(8,128)}, u32[]{:S(2)}) copy-start(f32[64,32]{0,1:T(8,128)} %param.43) | copy-start | bytes 24580
  1114.2 115.9 %copy-start.44 = (f32[64,32]{0,1:T(8,128)S(1)}, f32[64,32]{0,1:T(8,128)}, u32[]{:S(2)}) copy-start(f32[64,32]{0,1:T(8,128)} %param.50) | copy-start | bytes 24580
  1114.2 192.0 %copy-start.35 = (f32[3,32,64]{2,1,0:T(8,128)S(1)}, f32[3,32,64]{2,1,0:T(8,128)}, u32[]{:S(2)}) copy-start(f32[3,32,64]{2,1,0:T(8,128)} %param.35) | copy-start | bytes 73732
  1114.2 192.0 %copy-start.41 = (f32[3,32,64]{2,1,0:T(8,128)S(1)}, f32[3,32,64]{2,1,0:T(8,128)}, u32[]{:S(2)}) copy-start(f32[3,32,64]{2,1,0:T(8,128)} %param.42) | copy-start | bytes 73732
  1114.2 192.0 %copy-start.42 = (f32[3,32,64]{2,1,0:T(8,128)S(1)}, f32[3,32,64]{2,1,0:T(8,128)}, u32[]{:S(2)}) copy-start(f32[3,32,64]{2,1,0:T(8,128)} %param.49) | copy-start | bytes 73732
  1166.8 231.7 %copy-start.45 = (f32[6,32]{1,0:T(8,128)}, f32[6,32]{1,0:T(8,128)S(1)}, u32[]{:S(2)}) copy-start(f32[6,32]{1,0:T(8,128)S(1)} %copy.106) | copy-start | bytes 2308
  (86 other events, 546.2 us)
Sparse Core Ops, SparseCore 0:
  258.4 82.8 all-reduce.10
  398.6 82.7 all-reduce.12
  510.1 85.6 all-reduce.14
  599.9 61.9 reduce-scatter.11
  665.7 60.9 reduce-scatter.9
  1105.0 60.9 reduce-scatter.13
  1170.2 59.8 reduce-scatter.7
  1233.9 71.3 all-reduce.18
  1307.7 84.7 all-reduce.16
where the time goes:
time: 1420 us; the launch traced here: 1410 us
  waiting for transfers between devices  404 us (28%)
  matrix products  392 us (28%)
  other arithmetic  240 us (17%)
  blocking collectives  211 us (15%)
  local copies, waits for them, and re-layouts  113 us (8%)
  loops' own time  27.3 us (2%)
  between operations  17.7 us (1%)
    psum x4, waiting for transfers between devices, summed(): return lax.psum(partial_value, 'tensor')  243 us
    dot_general x8, matrix products, one_block(): jnp.einsum('qhd,khd->hqk', grad_block, value_heads, preferred_element_typ...  123 us
    convert_element_type x8, other arithmetic, one_block(): score_grad = (probs * (prob_grad - delta)).astype(jnp.bfloat16)  99.3 us
    unnamed x11, waiting for transfers between devices  97.6 us
    dot_general x8, matrix products, one_block(): jnp.einsum('hqk,qhd->khd', probs.astype(jnp.bfloat16), grad_block, prefer...  63.3 us
    reduce_scatter x1, waiting for transfers between devices, body(): lax.psum_scatter(grad_outward, 'dp', scatter_dimension=1, tiled=True)  62.7 us
    dot_general x16, matrix products, mask_scores(): jnp.einsum('qhd,khd->hqk', query_block, key_heads, preferred_element_type...  58.8 us
    and x16, other arithmetic, mask_scores(): allowed = (seg_block[:, None] == segment[None, :]) & key_open[None, :]  46.6 us
  transfers between devices with their start and end apart: 9, of which 6 were waited for; matrix products, arithmetic and copies ran while one was open for 33% of the time, Pallas kernels for 0%

commit v1 on v0

--- a/solution.py
+++ b/solution.py
@@ -53,7 +53,7 @@
 
 
 def summed(partial_value):
-    return lax.psum(partial_value, "tensor")
+    return jnp.sum(lax.all_gather(partial_value, "tensor"), axis=0)
 
 
 def mask_scores(query_block, key_heads, seg_block, segment, key_open):

time: 1420 us -> 1510 us (1.063)
  waiting for transfers between devices: 404 us -> 462 us
  other arithmetic: 240 us -> 277 us
    all_gather x0 -> x4, waiting for transfers between devices: none -> 303 us  [summed(): return jnp.sum(lax.all_gather(partial_value, 'tensor'), axis=0)]
    psum x4 -> x0, waiting for transfers between devices: 243 us -> none  [summed(): return lax.psum(partial_value, 'tensor')]
    reduce_sum x0 -> x4, other arithmetic: none -> 37.8 us  [summed(): return jnp.sum(lax.all_gather(partial_value, 'tensor'), axis=0)]
  transfers between devices with their start and end apart: 9 -> 9, of which waited for: 6 -> 6; matrix products, arithmetic and copies ran while one was open for 33% -> 32% of each run, Pallas kernels for 0% -> 0%
where the time goes in v1:
time: 1510 us; the launch traced here: 1500 us
  waiting for transfers between devices  462 us (31%)
  matrix products  393 us (26%)
  other arithmetic  277 us (18%)
  blocking collectives  212 us (14%)
  local copies, waits for them, and re-layouts  111 us (7%)
  loops' own time  27.1 us (2%)
  between operations  17.9 us (1%)
    all_gather x4, waiting for transfers between devices, summed(): return jnp.sum(lax.all_gather(partial_value, 'tensor'), axis=0)  303 us
    dot_general x8, matrix products, one_block(): jnp.einsum('qhd,khd->hqk', grad_block, value_heads, preferred_element_typ...  124 us
    convert_element_type x8, other arithmetic, one_block(): score_grad = (probs * (prob_grad - delta)).astype(jnp.bfloat16)  99.2 us
    unnamed x11, waiting for transfers between devices  97.3 us
    dot_general x8, matrix products, one_block(): jnp.einsum('hqk,qhd->khd', probs.astype(jnp.bfloat16), grad_block, prefer...  63.3 us
    reduce_scatter x1, waiting for transfers between devices, body(): lax.psum_scatter(grad_outward, 'dp', scatter_dimension=1, tiled=True)  62.4 us
    dot_general x16, matrix products, mask_scores(): jnp.einsum('qhd,khd->hqk', query_block, key_heads, preferred_element_type...  58.8 us
    while x96, local copies, waits for them, and re-layouts  46 us
  transfers between devices with their start and end apart: 9, of which 6 were waited for; matrix products, arithmetic and copies ran while one was open for 32% of the time, Pallas kernels for 0%

profile of v1, /device:TPU:0, one launch (start us, length us, event | category | flops | bytes accessed | tf_op | source)
XLA Modules:
  0.0 1501.0 jit_solution(12841025670019200616)
XLA Ops:
  8.1 22.1 %all-gather.4 = bf16[8,8,2]{1,2,0:T(2,128)(2,1)S(1)} all-gather(bf16[1,8,2]{1,2,0:T(2,128)(2,1)S(1)} %convert_bitcast_fusion.2), channel_id=1, replica_groups=mesh['dp'=8,'tensor'=4] {'dp'}, dimensions={0}, use_global_device_ids=true | all-gather | bytes 288 | tf_op jit(solution)/shard_map/all_gather | solution.py:195
  32.6 32.5 %all_gather.47 = bf16[64,256]{0,1:T(8,128)(2,1)} all-gather(bf16[64,32]{0,1:T(8,128)(2,1)S(1)} %convert_element_type.133), channel_id=1, replica_groups=mesh['dp'=8,'tensor'=4] {'dp'}, dimensions={1}, use_global_device_ids=true | all-gather | bytes 36864 | tf_op jit(solution)/shard_map/all_gather | solution.py:191
  65.1 30.6 %all_gather.45 = bf16[3,256,64]{2,1,0:T(8,128)(2,1)S(1)} all-gather(bf16[3,32,64]{2,1,0:T(8,128)(2,1)S(1)} %convert_element_type.125), channel_id=1, replica_groups=mesh['dp'=8,'tensor'=4] {'dp'}, dimensions={1}, use_global_device_ids=true | all-gather | bytes 110592 | tf_op jit(solution)/shard_map/all_gather | solution.py:190
  101.7 152.2 %while.27 = (s32[]{:T(128)}, bf16[8,512,64]{1,2,0:T(8,128)(2,1)S(1)}, f32[8,2,512]{2,1,0:T(2,128)}, s32[8]{0:T(128)S(1)}, s32[4096]{0:T(1024)}, /*index=5*/s32[1...) while((s32[]{:T(128)}, ...), condition=%wide.region_3.4_spmd, body=%wide.region_0.3_spmd.sunk | while | flops 591395840 | bytes 60221656 | solution.py:93
  258.4 17.4 %all-reduce = bf16[512]{0:T(512)(128)(2,1)S(1)} all-reduce(bf16[512]{0:T(512)(128)(2,1)S(1)} %dynamic-update-slice), channel_id=1, replica_groups=mesh['dp'=8,'tensor'=4] {'dp'}, use_global_device_ids=true, to_apply=%add | all-reduce | flops 512 | bytes 2048
  275.8 26.0 %all-gather.5 = bf16[8,32,6]{1,2,0:T(8,128)(2,1)S(1)} all-gather(bf16[1,32,6]{1,2,0:T(8,128)(2,1)S(1)} %convert_bitcast_fusion.1), channel_id=1, replica_groups=mesh['dp'=8,'tensor'=4] {'dp'}, dimensions={0}, use_global_device_ids=true | all-gather | bytes 3456 | tf_op jit(solution)/shard_map/all_gather | solution.py:194
  302.0 30.9 %all_gather.53 = bf16[512,256]{0,1:T(8,128)(2,1)S(1)} all-gather(bf16[512,32]{0,1:T(8,128)(2,1)S(1)} %convert_element_type.141), channel_id=1, replica_groups=mesh['dp'=8,'tensor'=4] {'dp'}, dimensions={1}, use_global_device_ids=true | all-gather | bytes 294912 | tf_op jit(solution)/shard_map/all_gather | solution.py:193
  332.9 30.7 %all_gather.51 = bf16[256,512]{1,0:T(8,128)(2,1)S(1)} all-gather(bf16[32,512]{1,0:T(8,128)(2,1)S(1)} %convert_element_type.137), channel_id=1, replica_groups=mesh['dp'=8,'tensor'=4] {'dp'}, dimensions={0}, use_global_device_ids=true | all-gather | bytes 294912 | tf_op jit(solution)/shard_map/all_gather | solution.py:192
  379.7 21.6 %multiply_convert_fusion.1 = (bf16[4096,512]{1,0:T(8,128)(2,1)S(1)}, f32[4096,512]{1,0:T(8,128)}, f32[4096,512]{1,0:T(8,128)}) fusion(f32[512]{0:T(512)S(1)} %convert_element_type.139, bf16[4096,256]{1,0:T(8,128)(2,1)S(1)} %fusion.36, bf16[256,512]{1,0:T(8,128)(2,1)S(1)} %all_gather.51), kind=kOutput, calls=%fused_computation.35 | convolution fusion | flops 1212153856 | bytes 23332864 | tf_op jit(solution)/shard_map/dot_general | solution.py:19
  407.2 102.9 %all-gather.13.cloned.1.call-done = f32[16384,256]{1,0:T(8,128)} async-done(((f32[4096,256]{1,0:T(8,128)}), f32[16384,256]{1,0:T(8,128)}) %all-gather.13.cloned.1.call-update) | async-done | bytes 16777232 | tf_op jit(solution)/shard_map/all_gather | solution.py:56
  559.7 94.5 %all-gather.15.cloned.1.call-done = f32[16384,256]{1,0:T(8,128)} async-done(((f32[4096,256]{1,0:T(8,128)}), f32[16384,256]{1,0:T(8,128)}) %all-gather.15.cloned.1.call-update) | async-done | bytes 16777232 | tf_op jit(solution)/shard_map/all_gather | solution.py:56
  677.7 476.8 %while.28 = (s32[]{:T(128)}, f32[4096,2,32]{0,2,1:T(8,128)S(1)}, f32[4096,2,32]{0,2,1:T(8,128)}, bf16[8,512,64]{1,2,0:T(8,128)(2,1)}, s32[8]{0:T(128)S(1)}, /*in...) while((s32[]{:T(128)}, f32[4096,2,32]{0,2,1:T(8,128)S(1)}, ...), condition=%wide.region_17.18_spmd.clone, body=%wide.region_15.17_spmd.clone.sunk | while | flops 1410399232 | bytes 220977600 | solution.py:141
  704.5 15.5 %multiply_reduce_fusion.7 = (f32[2,512]{1,0:T(2,128)S(1)}, f32[2,512,4096]{2,1,0:T(8,128)}) fusion(f32[2,512,4096]{2,1,0:T(8,128)} %copy-done, f32[2,512]{1,0:T(2,128)S(1)} %dynamic-slice_bitcast_fusion.2, pred[512,4096]{1,0:T(8,128)(4,1)} %compare_and_fusion.5, bf16[512,2,32]{0,2,1:T(8,128)(2,1)} %bitcast.199, ...), kind=kOutput, calls=%fused_computation.13.clone.1 | convolution fusion | flops 289405952 | bytes 36249600 | tf_op jit(solution)/shard_map/while/body/eval_jaxpr/qhd,khd->hqk/dot_general | solution.py:117
  719.9 12.4 multiply_convert_fusion.4
  764.1 15.5 %multiply_reduce_fusion.7 = (f32[2,512]{1,0:T(2,128)S(1)}, f32[2,512,4096]{2,1,0:T(8,128)}) fusion(f32[2,512,4096]{2,1,0:T(8,128)} %copy-done, f32[2,512]{1,0:T(2,128)S(1)} %dynamic-slice_bitcast_fusion.2, pred[512,4096]{1,0:T(8,128)(4,1)} %compare_and_fusion.5, bf16[512,2,32]{0,2,1:T(8,128)(2,1)} %bitcast.199, ...), kind=kOutput, calls=%fused_computation.13.clone.1 | convolution fusion | flops 289405952 | bytes 36249600 | tf_op jit(solution)/shard_map/while/body/eval_jaxpr/qhd,khd->hqk/dot_general | solution.py:117
  779.6 12.5 multiply_convert_fusion.4
  823.7 15.5 %multiply_reduce_fusion.7 = (f32[2,512]{1,0:T(2,128)S(1)}, f32[2,512,4096]{2,1,0:T(8,128)}) fusion(f32[2,512,4096]{2,1,0:T(8,128)} %copy-done, f32[2,512]{1,0:T(2,128)S(1)} %dynamic-slice_bitcast_fusion.2, pred[512,4096]{1,0:T(8,128)(4,1)} %compare_and_fusion.5, bf16[512,2,32]{0,2,1:T(8,128)(2,1)} %bitcast.199, ...), kind=kOutput, calls=%fused_computation.13.clone.1 | convolution fusion | flops 289405952 | bytes 36249600 | tf_op jit(solution)/shard_map/while/body/eval_jaxpr/qhd,khd->hqk/dot_general | solution.py:117
  839.2 12.4 multiply_convert_fusion.4
  883.3 15.5 %multiply_reduce_fusion.7 = (f32[2,512]{1,0:T(2,128)S(1)}, f32[2,512,4096]{2,1,0:T(8,128)}) fusion(f32[2,512,4096]{2,1,0:T(8,128)} %copy-done, f32[2,512]{1,0:T(2,128)S(1)} %dynamic-slice_bitcast_fusion.2, pred[512,4096]{1,0:T(8,128)(4,1)} %compare_and_fusion.5, bf16[512,2,32]{0,2,1:T(8,128)(2,1)} %bitcast.199, ...), kind=kOutput, calls=%fused_computation.13.clone.1 | convolution fusion | flops 289405952 | bytes 36249600 | tf_op jit(solution)/shard_map/while/body/eval_jaxpr/qhd,khd->hqk/dot_general | solution.py:117
  898.7 12.4 multiply_convert_fusion.4
  942.9 15.5 %multiply_reduce_fusion.7 = (f32[2,512]{1,0:T(2,128)S(1)}, f32[2,512,4096]{2,1,0:T(8,128)}) fusion(f32[2,512,4096]{2,1,0:T(8,128)} %copy-done, f32[2,512]{1,0:T(2,128)S(1)} %dynamic-slice_bitcast_fusion.2, pred[512,4096]{1,0:T(8,128)(4,1)} %compare_and_fusion.5, bf16[512,2,32]{0,2,1:T(8,128)(2,1)} %bitcast.199, ...), kind=kOutput, calls=%fused_computation.13.clone.1 | convolution fusion | flops 289405952 | bytes 36249600 | tf_op jit(solution)/shard_map/while/body/eval_jaxpr/qhd,khd->hqk/dot_general | solution.py:117
  958.3 12.4 multiply_convert_fusion.4
  1002.4 15.5 %multiply_reduce_fusion.7 = (f32[2,512]{1,0:T(2,128)S(1)}, f32[2,512,4096]{2,1,0:T(8,128)}) fusion(f32[2,512,4096]{2,1,0:T(8,128)} %copy-done, f32[2,512]{1,0:T(2,128)S(1)} %dynamic-slice_bitcast_fusion.2, pred[512,4096]{1,0:T(8,128)(4,1)} %compare_and_fusion.5, bf16[512,2,32]{0,2,1:T(8,128)(2,1)} %bitcast.199, ...), kind=kOutput, calls=%fused_computation.13.clone.1 | convolution fusion | flops 289405952 | bytes 36249600 | tf_op jit(solution)/shard_map/while/body/eval_jaxpr/qhd,khd->hqk/dot_general | solution.py:117
  1017.9 12.4 multiply_convert_fusion.4
  1062.0 15.5 %multiply_reduce_fusion.7 = (f32[2,512]{1,0:T(2,128)S(1)}, f32[2,512,4096]{2,1,0:T(8,128)}) fusion(f32[2,512,4096]{2,1,0:T(8,128)} %copy-done, f32[2,512]{1,0:T(2,128)S(1)} %dynamic-slice_bitcast_fusion.2, pred[512,4096]{1,0:T(8,128)(4,1)} %compare_and_fusion.5, bf16[512,2,32]{0,2,1:T(8,128)(2,1)} %bitcast.199, ...), kind=kOutput, calls=%fused_computation.13.clone.1 | convolution fusion | flops 289405952 | bytes 36249600 | tf_op jit(solution)/shard_map/while/body/eval_jaxpr/qhd,khd->hqk/dot_general | solution.py:117
  1077.5 12.4 multiply_convert_fusion.4
  1121.6 15.5 %multiply_reduce_fusion.7 = (f32[2,512]{1,0:T(2,128)S(1)}, f32[2,512,4096]{2,1,0:T(8,128)}) fusion(f32[2,512,4096]{2,1,0:T(8,128)} %copy-done, f32[2,512]{1,0:T(2,128)S(1)} %dynamic-slice_bitcast_fusion.2, pred[512,4096]{1,0:T(8,128)(4,1)} %compare_and_fusion.5, bf16[512,2,32]{0,2,1:T(8,128)(2,1)} %bitcast.199, ...), kind=kOutput, calls=%fused_computation.13.clone.1 | convolution fusion | flops 289405952 | bytes 36249600 | tf_op jit(solution)/shard_map/while/body/eval_jaxpr/qhd,khd->hqk/dot_general | solution.py:117
  1187.0 21.3 %all-reduce.4 = (f32[2,64]{1,0:T(2,128)S(1)}, f32[512]{0:T(512)S(1)}) all-reduce(f32[2,64]{1,0:T(2,128)S(1)} %pad_maximum_fusion.1, f32[512]{0:T(512)S(1)} %copy-done.57), channel_id=11, replica_groups=mesh['dp'=8,'tensor'=4] {'dp'}, use_global_device_ids=true, to_apply=%region_32.33.clone | all-reduce | flops 640 | bytes 5120
  1209.7 23.4 %reduce-scatter.14.cloned.1.call-done = f32[32,6]{1,0:T(8,128)} async-done(((f32[256,6]{1,0:T(8,128)}), f32[32,6]{1,0:T(8,128)}) %reduce-scatter.14.cloned.1.call-update) | async-done | bytes 784
  1234.6 62.4 %reduce-scatter.8.cloned.1.call-done = f32[64,32]{0,1:T(8,128)} async-done(((f32[64,256]{0,1:T(8,128)}), f32[64,32]{0,1:T(8,128)}) %reduce-scatter.8.cloned.1.call-update) | async-done | bytes 8208 | tf_op jit(solution)/shard_map/reduce_scatter | solution.py:269
  1298.3 73.5 %all-reduce.7.cloned.1.call-done = f32[3,256,64]{2,0,1:T(4,128)} async-done(((f32[3,256,64]{2,0,1:T(4,128)}), f32[3,256,64]{2,0,1:T(4,128)}) %all-reduce.7.cloned.1.call-update) | async-done | bytes 196624
  1373.4 105.3 %all-gather.17.cloned.1.call-done = f32[16384,256]{1,0:T(8,128)} async-done(((f32[4096,256]{1,0:T(8,128)}), f32[16384,256]{1,0:T(8,128)}) %all-gather.17.cloned.1.call-update) | async-done | bytes 16777232 | tf_op jit(solution)/shard_map/all_gather | solution.py:56
  (477 shorter events, 550.3 us)
Async XLA Ops:
  7.2 91.4 %copy-start.12 = (bf16[4096,256]{1,0:T(8,128)(2,1)S(1)}, bf16[4096,256]{1,0:T(8,128)(2,1)}, u32[]{:S(2)}) copy-start(bf16[4096,256]{1,0:T(8,128)(2,1)} %param.30) | copy-start | bytes 6291460
  7.2 356.4 %all-gather.11.cloned.1.call-start = ((), (), s32[]{:S(2)}) async-start(), calls=%async_computation.7 | async-start | bytes 20971520 | tf_op jit(solution)/shard_map/all_gather | solution.py:56
  101.7 152.3 %copy-start.29 = (bf16[64,256]{0,1:T(8,128)(2,1)S(1)}, bf16[64,256]{0,1:T(8,128)(2,1)}, u32[]{:S(2)}) copy-start(bf16[64,256]{0,1:T(8,128)(2,1)} %all_gather.47) | copy-start | bytes 98308
  254.0 21.9 %copy-start.46 = (f32[6,32]{1,0:T(8,128)S(1)}, f32[6,32]{1,0:T(8,128)}, u32[]{:S(2)}) copy-start(f32[6,32]{1,0:T(8,128)} %param.39) | copy-start | bytes 2308
  254.0 48.0 %copy-start.33 = (f32[32,512]{1,0:T(8,128)S(1)}, f32[32,512]{1,0:T(8,128)}, u32[]{:S(2)}) copy-start(f32[32,512]{1,0:T(8,128)} %param.37) | copy-start | bytes 196612
  254.0 48.0 %copy-start.31 = (f32[512,32]{0,1:T(8,128)S(1)}, f32[512,32]{0,1:T(8,128)}, u32[]{:S(2)}) copy-start(f32[512,32]{0,1:T(8,128)} %param.38) | copy-start | bytes 196612
  256.8 253.2 %all-gather.13.cloned.1.call-start = ((), (), s32[]{:S(2)}) async-start(), calls=%async_computation.8 | async-start | bytes 20971520 | tf_op jit(solution)/shard_map/all_gather | solution.py:56
  379.7 21.6 %copy-start.24 = (bf16[4096,256]{1,0:T(8,128)(2,1)}, bf16[4096,256]{1,0:T(8,128)(2,1)S(1)}, u32[]{:S(2)}) copy-start(bf16[4096,256]{1,0:T(8,128)(2,1)S(1)} %fusion.36) | copy-start | bytes 6291460
  406.7 247.5 %all-gather.15.cloned.1.call-start = ((), (), s32[]{:S(2)}) async-start(), calls=%async_computation.9 | async-start | bytes 20971520 | tf_op jit(solution)/shard_map/all_gather | solution.py:56
  548.1 635.6 %reduce-scatter.12.cloned.1.call-start = ((), (), s32[]{:S(2)}) async-start(), calls=%async_computation.6 | async-start | bytes 589824 | tf_op jit(solution)/shard_map/reduce_scatter | solution.py:271
  553.7 631.5 %reduce-scatter.10.cloned.1.call-start = ((), (), s32[]{:S(2)}) async-start(), calls=%async_computation.5 | async-start | bytes 589824 | tf_op jit(solution)/shard_map/reduce_scatter | solution.py:270
  559.7 673.5 %reduce-scatter.14.cloned.1.call-start = ((), (), s32[]{:S(2)}) async-start(), calls=%async_computation.11 | async-start | bytes 147456
  704.5 15.5 %copy-start.1 = (pred[512,4096]{1,0:T(8,128)(4,1)S(1)}, pred[512,4096]{1,0:T(8,128)(4,1)}, u32[]{:S(2)}) copy-start(pred[512,4096]{1,0:T(8,128)(4,1)} %compare_and_fusion.5) | copy-start | bytes 6291460 | tf_op jit(solution)/shard_map/while
  1172.2 124.8 %reduce-scatter.8.cloned.1.call-start = ((), (), s32[]{:S(2)}) async-start(), calls=%async_computation.4 | async-start | bytes 147456 | tf_op jit(solution)/shard_map/reduce_scatter | solution.py:269
  1172.9 198.9 %all-reduce.7.cloned.1.call-start = ((), (), s32[]{:S(2)}) async-start(), calls=%async_computation.12 | async-start | bytes 1048576
  1176.3 302.4 %all-gather.17.cloned.1.call-start = ((), (), s32[]{:S(2)}) async-start(), calls=%async_computation.10 | async-start | bytes 20971520 | tf_op jit(solution)/shard_map/all_gather | solution.py:56
  1181.2 27.1 %copy-start.62 = (f32[64]{0:T(128)S(1)}, f32[64]{0:T(128)}, u32[]{:S(2)}) copy-start(f32[64]{0:T(128)} %param.41) | copy-start | bytes 772
  1181.3 27.1 %copy-start.63 = (f32[64]{0:T(128)S(1)}, f32[64]{0:T(128)}, u32[]{:S(2)}) copy-start(f32[64]{0:T(128)} %param.48) | copy-start | bytes 772
  1181.3 27.1 %copy-start.64 = (f32[64]{0:T(128)S(1)}, f32[64]{0:T(128)}, u32[]{:S(2)}) copy-start(f32[64]{0:T(128)} %param.55) | copy-start | bytes 772
  1181.3 27.7 %copy-start.58 = (f32[2,8]{1,0:T(2,128)S(1)}, f32[2,8]{1,0:T(2,128)}, u32[]{:S(2)}) copy-start(f32[2,8]{1,0:T(2,128)} %param.40) | copy-start | bytes 196
  1181.3 27.7 %copy-start.59 = (f32[2,8]{1,0:T(2,128)S(1)}, f32[2,8]{1,0:T(2,128)}, u32[]{:S(2)}) copy-start(f32[2,8]{1,0:T(2,128)} %param.47) | copy-start | bytes 196
  1181.3 27.7 %copy-start.60 = (f32[2,8]{1,0:T(2,128)S(1)}, f32[2,8]{1,0:T(2,128)}, u32[]{:S(2)}) copy-start(f32[2,8]{1,0:T(2,128)} %param.54) | copy-start | bytes 196
  1181.3 52.6 %copy-start.47 = (f32[6,32]{1,0:T(8,128)S(1)}, f32[6,32]{1,0:T(8,128)}, u32[]{:S(2)}) copy-start(f32[6,32]{1,0:T(8,128)} %param.39) | copy-start | bytes 2308
  1181.3 52.6 %copy-start.53 = (f32[6,32]{1,0:T(8,128)S(1)}, f32[6,32]{1,0:T(8,128)}, u32[]{:S(2)}) copy-start(f32[6,32]{1,0:T(8,128)} %param.46) | copy-start | bytes 2308
  1181.3 52.6 %copy-start.54 = (f32[6,32]{1,0:T(8,128)S(1)}, f32[6,32]{1,0:T(8,128)}, u32[]{:S(2)}) copy-start(f32[6,32]{1,0:T(8,128)} %param.53) | copy-start | bytes 2308
  1181.3 115.6 %copy-start.40 = (f32[64,32]{0,1:T(8,128)S(1)}, f32[64,32]{0,1:T(8,128)}, u32[]{:S(2)}) copy-start(f32[64,32]{0,1:T(8,128)} %param.36) | copy-start | bytes 24580
  1181.4 115.6 %copy-start.43 = (f32[64,32]{0,1:T(8,128)S(1)}, f32[64,32]{0,1:T(8,128)}, u32[]{:S(2)}) copy-start(f32[64,32]{0,1:T(8,128)} %param.43) | copy-start | bytes 24580
  1181.4 115.6 %copy-start.44 = (f32[64,32]{0,1:T(8,128)S(1)}, f32[64,32]{0,1:T(8,128)}, u32[]{:S(2)}) copy-start(f32[64,32]{0,1:T(8,128)} %param.50) | copy-start | bytes 24580
  1181.4 191.3 %copy-start.35 = (f32[3,32,64]{2,1,0:T(8,128)S(1)}, f32[3,32,64]{2,1,0:T(8,128)}, u32[]{:S(2)}) copy-start(f32[3,32,64]{2,1,0:T(8,128)} %param.35) | copy-start | bytes 73732
  1181.4 191.3 %copy-start.41 = (f32[3,32,64]{2,1,0:T(8,128)S(1)}, f32[3,32,64]{2,1,0:T(8,128)}, u32[]{:S(2)}) copy-start(f32[3,32,64]{2,1,0:T(8,128)} %param.42) | copy-start | bytes 73732
  1181.4 191.3 %copy-start.42 = (f32[3,32,64]{2,1,0:T(8,128)S(1)}, f32[3,32,64]{2,1,0:T(8,128)}, u32[]{:S(2)}) copy-start(f32[3,32,64]{2,1,0:T(8,128)} %param.49) | copy-start | bytes 73732
  1233.9 254.1 %copy-start.45 = (f32[6,32]{1,0:T(8,128)}, f32[6,32]{1,0:T(8,128)S(1)}, u32[]{:S(2)}) copy-start(f32[6,32]{1,0:T(8,128)S(1)} %copy.106) | copy-start | bytes 2308
  (86 other events, 543.6 us)
Sparse Core Ops, SparseCore 0:
  256.9 103.2 all-gather.10
  406.8 103.2 all-gather.12
  548.2 105.9 all-gather.14
  657.9 61.8 reduce-scatter.11
  724.0 60.9 reduce-scatter.9
  1172.3 60.8 reduce-scatter.13
  1237.0 59.8 reduce-scatter.7
  1300.3 71.4 all-reduce.6
  1373.4 105.1 all-gather.16
